TPU v7x, 32 devices: a whole 2x2x4 slice. The times are simulated.
32 devices in a mesh: dp: 8 (over y, x, core), neg: 4 (over z).
Axes of the slice: x: 2, y: 2, z: 4, core: 2. Of those that a mesh axis runs over, the one named last changes fastest.
Arguments:
- img_features: bfloat16 [64, 256, 1024], P(('dp', 'neg'))
- txt_features: bfloat16 [64, 64, 1024], P(('dp', 'neg'))
- w_img: bfloat16 [1024, 256], replicated
- w_txt: bfloat16 [1024, 256], replicated
- cap_len: int32 [64], P(('dp', 'neg')), may hold values from 16 to 64
- pairs: int32 [8, 8], P('dp'), may hold values from 0 to 7, each once within a row
Outputs:
- grad_img_features: bfloat16 [64, 256, 1024], P(('dp', 'neg'))
- grad_txt_features: bfloat16 [64, 64, 1024], P(('dp', 'neg'))
- grad_w_img: float32 [1024, 256], P('dp')
- grad_w_txt: float32 [1024, 256], P('dp')
Inputs may be any that keep to these rules, and one draw needn't show every extreme that they name: `pairs`: each row is a permutation of 0 to 7.
All inputs are finite; a program needn't handle non-finite values.
Results may differ from a plain program's by a relative error of at most 0.011.
Values may be sent and summed in bfloat16 or wider, within the bound.
A program may use at most 64 MiB of HBM per device.

v0:
```python
import functools

import jax
import jax.numpy as jnp
from jax import lax
from jax.experimental import pallas as pl
from jax.experimental.pallas import tpu as pltpu
from jax.sharding import PartitionSpec as P

TOKEN_SCALE = 100.0
PAIR_SCALE = 50.0
EPSILON = 1e-06
MARK = 4.0
LOW = -1e30
VMEM_BYTES = 60 * 1024 * 1024
BF = jnp.bfloat16
F32 = jnp.float32
MESH = pl.DeviceIdType.MESH


def nn(a, b):
    return lax.dot_general(a, b, (((1,), (0,)), ((), ())), preferred_element_type=F32)


def nt(a, b):
    return lax.dot_general(a, b, (((1,), (1,)), ((), ())), preferred_element_type=F32)


def unit_rows(projected):
    inverse = lax.rsqrt(jnp.sum(projected * projected, axis=-1, keepdims=True) + EPSILON)
    return projected * inverse, inverse


def back_unit(gradient, unit, inverse):
    return (gradient - unit * jnp.sum(unit * gradient, axis=-1, keepdims=True)) * inverse


class Exchange:
    def __init__(self, me, n, device, slots, send, recv, line=True):
        self.me, self.n, self.device, self.line = me, n, device, line
        self.slots, self.send, self.recv = slots, send, recv
        self.started = []

    def peer(self, offset):
        if not self.line:
            return lax.rem(self.me + offset, self.n)
        upper = lax.div(self.me * 2, self.n)
        k = upper * (offset - 1) + (1 - upper) * (self.n - 1 - offset)
        return k + lax.div(k + self.n - self.me, self.n)

    def start(self, offset, source):
        copy = pltpu.make_async_remote_copy(
            src_ref=source,
            dst_ref=self.slots.at[self.me],
            send_sem=self.send.at[offset],
            recv_sem=self.recv.at[self.me],
            device_id=self.device(self.peer(offset)),
            device_id_type=MESH,
        )
        copy.start()
        self.started.append(copy)

    def take(self, offset):
        other = self.peer(offset)
        pltpu.make_async_remote_copy(
            src_ref=self.slots.at[other],
            dst_ref=self.slots.at[other],
            send_sem=self.send.at[offset],
            recv_sem=self.recv.at[other],
            device_id=self.device(other),
            device_id_type=MESH,
        ).wait_recv()
        return other

    def finish(self):
        for copy in self.started:
            copy.wait_send()


def kernel(
    dims,
    img_hbm, txt_hbm, wi_hbm, wt_hbm, cap, pairs,
    fi_hbm, ft_hbm, gi_hbm, gt_hbm,
    img, txt, wi, wt, img_t, txt_t,
    img_unit, img_inv, img_half, txt_unit, txt_inv,
    text_all, expo, total, logit_all, sg, terms, own_term, term_in,
    img_back, txt_back, wg, core_out, core_in, plane_out, plane_own, plane_in,
    part, part_out, ring_in, full, fi, ft, grads,
    load_sem, save_sem,
    text_s, text_r, logit_s, logit_r, term_s, term_r,
    core_s, core_r, plane_s, plane_r, ring_s, ring_r, full_s, full_r,
):
    L, PI, T, D, W, N, NDP = dims
    H = NDP // 2
    r = D // NDP
    rows_i, rows_t = L * PI, L * T
    dp = lax.axis_index("dp")
    me = lax.axis_index("neg")
    core = lax.rem(dp, 2)
    chip = lax.div(dp, 2)
    split = r % (16 * N) == 0
    rr = r // N if split else r

    loads = [
        pltpu.make_async_copy(source, target, load_sem.at[i])
        for i, (source, target) in enumerate(
            ((txt_hbm, txt), (wt_hbm, wt), (wi_hbm, wi), (img_hbm, img))
        )
    ]
    for load in loads:
        load.start()

    def on_neg(k):
        return (dp, k)

    def on_plane(k):
        return (k * 2 + core, me)

    barrier = pltpu.get_barrier_semaphore()
    for o in range(1, N):
        pl.semaphore_signal(barrier, inc=1, device_id=on_neg(lax.rem(me + o, N)), device_id_type=MESH)
    for o in range(1, H):
        pl.semaphore_signal(
            barrier, inc=1, device_id=on_plane(lax.rem(chip + o, H)), device_id_type=MESH
        )
    mate = (chip * 2 + 1 - core, me)
    pl.semaphore_signal(barrier, inc=1, device_id=mate, device_id_type=MESH)

    loads[0].wait()
    loads[1].wait()
    unit, inverse = unit_rows(nn(txt[...], wt[...]))
    txt_unit[...] = unit
    txt_inv[...] = inverse
    place = lax.broadcasted_iota(jnp.int32, (T, W), 0)
    for c in range(L):
        text_all[me, c * T:(c + 1) * T, :] = jnp.where(
            place < cap[c], unit[c * T:(c + 1) * T], MARK
        ).astype(BF)
    pl.semaphore_wait(barrier, N - 1 + H - 1 + 1)
    text_x = Exchange(me, N, on_neg, text_all, text_s, text_r)
    for o in range(1, N):
        text_x.start(o, text_all.at[me])

    loads[2].wait()
    loads[3].wait()
    for i in range(L):
        rows = slice(i * PI, (i + 1) * PI)
        unit, inverse = unit_rows(nn(img[rows, :], wi[...]))
        img_unit[rows, :] = unit
        img_inv[rows, :] = inverse
        img_half[rows, :] = unit.astype(BF)

    def transpose_features(features, features_t, start, size):
        step = max(256, r)
        for d in range(0, D, step):
            turned = features[start:start + size, d:d + step].T
            for k in range(d // r, (d + step) // r):
                at = k // 2 * r
                features_t[k % 2, at:at + r, start:start + size] = turned[k * r - d:(k + 1) * r - d]

    lane = lax.broadcasted_iota(jnp.int32, (8, 128), 1)
    line = lax.broadcasted_iota(jnp.int32, (8, 128), 0)

    def pool(j):
        text = text_all[j]
        marks = text[:, 0:128].astype(F32)
        marks = jnp.concatenate([marks] * (rows_i // 128), axis=1)
        scores = jnp.where(marks < 2.0, TOKEN_SCALE * nt(text, img_half[...]), LOW)
        scores = scores.reshape(L, T, rows_i)
        peaks = jnp.max(scores, axis=1, keepdims=True)
        expos = jnp.exp(scores - peaks)
        totals = jnp.sum(expos, axis=1)
        expo[j] = expos.reshape(rows_t, rows_i)
        total[j] = jnp.concatenate([totals, jnp.ones((8 - L, rows_i), F32)], axis=0)
        pooled = peaks[:, 0, :] + jnp.log(totals)
        pooled = jnp.concatenate([pooled, jnp.zeros((8 - L, rows_i), F32)], axis=0)
        tile = jnp.full((8, 128), LOW, F32)
        for i in range(L):
            mean = jnp.sum(pooled[:, i * PI:(i + 1) * PI], axis=1, keepdims=True)
            mean = mean * (PAIR_SCALE / (TOKEN_SCALE * PI))
            tile = jnp.where((lane == i) & (line < L), mean, tile)
        logit_all[me, j] = tile

    pool(me)
    transpose_features(img, img_t, 0, PI)
    for o in reversed(range(1, N)):
        pool(text_x.take(o))
    logit_x = Exchange(me, N, on_neg, logit_all, logit_s, logit_r)
    for o in range(1, N):
        logit_x.start(o, logit_all.at[me])
    transpose_features(txt, txt_t, 0, rows_t)
    for i in range(1, L):
        transpose_features(img, img_t, i * PI, PI)
    own = logit_all[me]
    row_top = jnp.max(jnp.max(own, axis=0), axis=0, keepdims=True)
    row_exp = jnp.exp(own - row_top[None])
    row_prob = row_exp / jnp.sum(jnp.sum(row_exp, axis=0), axis=0, keepdims=True)[None]
    caption = lax.broadcasted_iota(jnp.int32, (N, 8, 128), 0) * L + lax.broadcasted_iota(
        jnp.int32, (N, 8, 128), 1
    )
    lanes = lax.broadcasted_iota(jnp.int32, (N, 8, 128), 2)
    target = jnp.zeros((N, 8, 128), F32)
    for i in range(L):
        target = jnp.where((lanes == i) & (caption == pairs[0, me * L + i]), 1.0, target)
    for o in range(1, N):
        logit_x.take(o)
    everyone = logit_all[...]
    col_top = jnp.max(jnp.max(everyone, axis=0), axis=-1, keepdims=True)
    col_sum = jnp.sum(
        jnp.sum(jnp.exp(everyone - col_top[None]), axis=0), axis=-1, keepdims=True
    )
    col_prob = jnp.exp(own - col_top) / col_sum
    pair_grad = (row_prob + col_prob - 2.0 * target) * (PAIR_SCALE / (2.0 * N * L * PI))
    own_logits = logit_all.at[me]
    logit_x.finish()
    own_logits[...] = pair_grad

    term_x = Exchange(me, N, on_neg, term_in, term_s, term_r)
    for o in list(range(1, N)) + [0]:
        j = term_x.peer(o) if o else me
        pair = own_logits[j]
        spread = jnp.concatenate(
            [jnp.broadcast_to(pair[:, i:i + 1], (8, PI)) for i in range(L)], axis=1
        )
        factor = spread / total[j]
        shares = []
        for c in range(L):
            shares.append((expo[j, c * T:(c + 1) * T, :] * factor[c:c + 1, :]).astype(BF))
        share = jnp.concatenate(shares, axis=0)
        sg[j] = share
        term = nn(share, img_half[...])
        if o == 0:
            own_term[...] = term
        else:
            terms[o] = term.astype(BF)
            term_x.start(o, terms.at[o])

    texts = text_all[...].reshape(N * rows_t, W)
    for i in range(L):
        rows = slice(i * PI, (i + 1) * PI)
        grad = nn(sg[:, :, rows].reshape(N * rows_t, PI).T, texts)
        img_back[rows, :] = back_unit(grad, img_unit[rows, :], img_inv[rows, :]).astype(BF)

    cores = []

    def core_copy(m):
        return pltpu.make_async_remote_copy(
            src_ref=core_out.at[m],
            dst_ref=core_in.at[m],
            send_sem=core_s.at[m],
            recv_sem=core_r.at[m],
            device_id=mate,
            device_id_type=MESH,
        )

    def weight_grad(m, features_t, back):
        step = max(256, r)
        for d in range(0, H * r, step):
            out = nn(features_t[1 - core, d:d + step, :], back[...]).astype(BF)
            core_out[m, d // r:(d + step) // r] = out.reshape(step // r, r, W)
        copy = core_copy(m)
        copy.start()
        cores.append(copy)
        for d in range(0, H * r, step):
            out = nn(features_t[core, d:d + step, :], back[...])
            wg[m, d // r:(d + step) // r] = out.reshape(step // r, r, W)

    planes = [
        Exchange(chip, H, on_plane, plane_in.at[m], plane_s.at[m], plane_r.at[m], line=False) for m in range(2)
    ]
    rings = [Exchange(me, N, on_neg, ring_in.at[m], ring_s.at[m], ring_r.at[m]) for m in range(2)]
    fulls = [Exchange(me, N, on_neg, full.at[m], full_s.at[m], full_r.at[m]) for m in range(2)]

    def plane_send(m):
        cores[m].wait_recv()
        for o in range(1, H):
            k = planes[m].peer(o)
            plane_out[m, o] = (wg[m, k] + core_in[m, k].astype(F32)).astype(BF)
            planes[m].start(o, plane_out.at[m, o])
        plane_own[m] = wg[m, chip] + core_in[m, chip].astype(F32)

    def ring_send(m):
        value = plane_own[m]
        for o in range(1, H):
            value = value + plane_in[m, planes[m].take(o)].astype(F32)
        if split:
            value = value.reshape(N, rr, W)
            part[m] = value
            part_out[m] = value.astype(BF)
            for o in range(1, N):
                rings[m].start(o, part_out.at[m, rings[m].peer(o)])
        else:
            ring_in[m, me] = value.astype(BF)
            for o in range(1, N):
                rings[m].start(o, ring_in.at[m, me])

    def full_send(m):
        if split:
            value = part[m, me]
            for o in range(1, N):
                value = value + ring_in[m, rings[m].take(o)].astype(F32)
            full[m, me] = value.astype(BF)
            for o in range(1, N):
                fulls[m].start(o, full.at[m, me])

    saves = []

    def save(i, source, target):
        copy = pltpu.make_async_copy(source, target, save_sem.at[i])
        copy.start()
        saves.append(copy)

    def result(m, out):
        if split:
            for o in range(1, N):
                fulls[m].take(o)
            grads[m] = full[m].astype(F32).reshape(r, W)
        else:
            for o in range(1, N):
                rings[m].take(o)
            grads[m] = jnp.sum(ring_in[m].astype(F32), axis=0)
        save(2 + m, grads.at[m], out)

    weight_grad(0, img_t, img_back)
    fi[0:PI, :] = nt(img_back[0:PI, :], wi[...]).astype(BF)
    plane_send(0)

    grad = own_term[...]
    for o in range(1, N):
        grad = grad + term_in[term_x.take(o)].astype(F32)
    txt_back[...] = back_unit(grad, txt_unit[...], txt_inv[...]).astype(BF)
    weight_grad(1, txt_t, txt_back)
    ring_send(0)
    plane_send(1)
    ft[...] = nt(txt_back[...], wt[...]).astype(BF)
    save(1, ft, ft_hbm)
    full_send(0)
    for i in range(1, L):
        rows = slice(i * PI, (i + 1) * PI)
        fi[rows, :] = nt(img_back[rows, :], wi[...]).astype(BF)
    save(0, fi, fi_hbm)
    ring_send(1)
    result(0, gi_hbm)
    full_send(1)
    result(1, gt_hbm)

    for copy in cores:
        copy.wait_send()
    for copy in saves:
        copy.wait()
    for exchange in [text_x, term_x] + planes + rings + fulls:
        exchange.finish()


def write_out(*refs):
    sources, targets, held, in_sem, out_sem = refs[:4], refs[4:8], refs[8:12], refs[12], refs[13]
    loads, saves = [], []
    for source, target, hold in zip(sources, targets, held):
        rows = source.shape[0]
        step = rows // 4 if rows % 64 == 0 and source.dtype == BF else rows
        for at in range(0, rows, step):
            piece, i = pl.ds(at, step), len(loads)
            loads.append(pltpu.make_async_copy(source.at[piece], hold.at[piece], in_sem.at[i]))
            saves.append(pltpu.make_async_copy(hold.at[piece], target.at[piece], out_sem.at[i]))
    for load in loads:
        load.start()
    for load, save in zip(loads, saves):
        load.wait()
        save.start()
    for save in saves:
        save.wait()


def shards(n_dp, n_neg, img_features, txt_features, w_img, w_txt, cap_len, pairs):
    L, PI, D = img_features.shape
    T = txt_features.shape[1]
    W = w_img.shape[1]
    N, H, r = n_neg, n_dp // 2, D // n_dp
    rows_i, rows_t = L * PI, L * T
    rr = r // N if r % (16 * N) == 0 else r
    vmem, dma = pltpu.VMEM, pltpu.SemaphoreType.DMA
    scratch = [
        vmem((rows_i, D), BF), vmem((rows_t, D), BF), vmem((D, W), BF), vmem((D, W), BF),
        vmem((2, H * r, rows_i), BF), vmem((2, H * r, rows_t), BF),
        vmem((rows_i, W), F32), vmem((rows_i, 1), F32), vmem((rows_i, W), BF),
        vmem((rows_t, W), F32), vmem((rows_t, 1), F32),
        vmem((N, rows_t, W), BF), vmem((N, rows_t, rows_i), F32), vmem((N, 8, rows_i), F32),
        vmem((N, N, 8, 128), F32), vmem((N, rows_t, rows_i), BF),
        vmem((N, rows_t, W), BF), vmem((rows_t, W), F32), vmem((N, rows_t, W), BF),
        vmem((rows_i, W), BF), vmem((rows_t, W), BF),
        vmem((2, H, r, W), F32), vmem((2, H, r, W), BF), vmem((2, H, r, W), BF),
        vmem((2, H, r, W), BF), vmem((2, r, W), F32), vmem((2, H, r, W), BF),
        vmem((2, N, rr, W), F32), vmem((2, N, rr, W), BF),
        vmem((2, N, rr, W), BF), vmem((2, N, rr, W), BF),
        vmem((rows_i, D), BF), vmem((rows_t, D), BF), vmem((2, r, W), F32),
        dma((4,)), dma((4,)),
        dma((N,)), dma((N,)), dma((N,)), dma((N,)), dma((N,)), dma((N,)),
        dma((2,)), dma((2,)), dma((2, H)), dma((2, H)),
        dma((2, N)), dma((2, N)), dma((2, N)), dma((2, N)),
    ]
    shapes = (
        jax.ShapeDtypeStruct((rows_i, D), BF),
        jax.ShapeDtypeStruct((rows_t, D), BF),
        jax.ShapeDtypeStruct((r, W), F32),
        jax.ShapeDtypeStruct((r, W), F32),
    )
    results = pl.pallas_call(
        functools.partial(kernel, (L, PI, T, D, W, N, n_dp)),
        out_shape=shapes,
        in_specs=[pl.BlockSpec(memory_space=pltpu.HBM)] * 4
        + [pl.BlockSpec(memory_space=pltpu.SMEM)] * 2,
        out_specs=(pl.BlockSpec(memory_space=pltpu.HBM),) * 4,
        scratch_shapes=scratch,
        compiler_params=pltpu.CompilerParams(
            collective_id=0, has_side_effects=True, vmem_limit_bytes=VMEM_BYTES
        ),
    )(
        img_features.reshape(rows_i, D),
        txt_features.reshape(rows_t, D),
        w_img,
        w_txt,
        cap_len,
        pairs,
    )
    feat_img, feat_txt, final_img, final_txt = pl.pallas_call(
        write_out,
        out_shape=shapes,
        in_specs=[pl.BlockSpec(memory_space=pl.ANY)] * 4,
        out_specs=(pl.BlockSpec(memory_space=pltpu.HBM),) * 4,
        scratch_shapes=[vmem(shape.shape, shape.dtype) for shape in shapes]
        + [dma((16,)), dma((16,))],
        compiler_params=pltpu.CompilerParams(vmem_limit_bytes=VMEM_BYTES),
    )(*results)
    return (
        feat_img.reshape(img_features.shape),
        feat_txt.reshape(txt_features.shape),
        final_img,
        final_txt,
    )


def solution(mesh):
    in_specs = (
        P(("dp", "neg"), None, None),
        P(("dp", "neg"), None, None),
        P(),
        P(),
        P(("dp", "neg")),
        P("dp", None),
    )
    out_specs = (
        P(("dp", "neg"), None, None),
        P(("dp", "neg"), None, None),
        P("dp", None),
        P("dp", None),
    )
    body = functools.partial(shards, mesh.shape["dp"], mesh.shape["neg"])
    return jax.shard_map(body, mesh=mesh, in_specs=in_specs, out_specs=out_specs, check_vma=False)
```

profile of v0, /device:TPU:0, one launch (start us, length us, event | category | flops | bytes accessed | tf_op | source)
XLA Modules:
  0.0 41.5 jit_solution(3518332150793777473)
XLA Ops:
  0.6 38.5 %shard_map.93 = (bf16[512,1024]{1,0:T(8,128)(2,1)}, bf16[128,1024]{1,0:T(8,128)(2,1)}, f32[128,256]{1,0:T(8,128)}, f32[128,256]{1,0:T(8,128)}) custom-call(bf16[512,1024]{1,0:T(8,128)(2,1)} %bitcast.4, bf16[128,1024]{1,0:T(8,128)(2,1)} %bitcast.5, bf16[1024,256]{1,0:T(8,128)(2,1)} %wi_hbm.1, bf16[1024,256]{1,0:T(8,128)(2,1)} %wt_hbm.1, s32[2]{0:T(128)} %cap.1, ...), custom_call_target="tpu_custom_call" | custom-call | tf_op jit(solution)/shard_map/pallas_call | solution.py:407
  39.1 2.4 %shard_map.94 = (bf16[512,1024]{1,0:T(8,128)(2,1)}, bf16[128,1024]{1,0:T(8,128)(2,1)}, f32[128,256]{1,0:T(8,128)}, f32[128,256]{1,0:T(8,128)}) custom-call(bf16[512,1024]{1,0:T(8,128)(2,1)} %get-tuple-element.12.refs_0_, bf16[128,1024]{1,0:T(8,128)(2,1)} %get-tuple-element.13.refs_1_, f32[128,256]{1,0:T(8,128)} %get-tuple-element.14.refs_2_, ...), custom_call_target="tpu_custom_call" | custom-call | tf_op jit(solution)/shard_map/pallas_call | solution.py:425
where the time goes:
time: 41.6 us; the launch traced here: 41.5 us
  Pallas kernels  40.8 us (98%)
  between operations  0.64 us (2%)
    pallas_call x1, Pallas kernels, shards(): pl.pallas_call(functools.partial(kernel, (L, PI, T, D, W, N, n_dp)), out_...  38.5 us
    pallas_call x1, Pallas kernels, shards(): pl.pallas_call(write_out, out_shape=shapes, in_specs=[pl.BlockSpec(memory...  2.36 us

commit v1 on v0

--- a/solution.py
+++ b/solution.py
@@ -161,7 +161,7 @@
     lane = lax.broadcasted_iota(jnp.int32, (8, 128), 1)
     line = lax.broadcasted_iota(jnp.int32, (8, 128), 0)
 
-    def pool(j):
+    def pool(j, tile):
         text = text_all[j]
         marks = text[:, 0:128].astype(F32)
         marks = jnp.concatenate([marks] * (rows_i // 128), axis=1)
@@ -174,53 +174,64 @@
         total[j] = jnp.concatenate([totals, jnp.ones((8 - L, rows_i), F32)], axis=0)
         pooled = peaks[:, 0, :] + jnp.log(totals)
         pooled = jnp.concatenate([pooled, jnp.zeros((8 - L, rows_i), F32)], axis=0)
-        tile = jnp.full((8, 128), LOW, F32)
         for i in range(L):
             mean = jnp.sum(pooled[:, i * PI:(i + 1) * PI], axis=1, keepdims=True)
             mean = mean * (PAIR_SCALE / (TOKEN_SCALE * PI))
-            tile = jnp.where((lane == i) & (line < L), mean, tile)
-        logit_all[me, j] = tile
-
-    pool(me)
-    transpose_features(img, img_t, 0, PI)
+            tile = jnp.where((lane == j * L + i) & (line < L), mean, tile)
+        return tile
+
+    tile = pool(me, jnp.full((8, 128), LOW, F32))
+    for i in range(L):
+        transpose_features(img, img_t, i * PI, PI)
     for o in reversed(range(1, N)):
-        pool(text_x.take(o))
+        tile = pool(text_x.take(o), tile)
+    logit_all[me] = tile
     logit_x = Exchange(me, N, on_neg, logit_all, logit_s, logit_r)
     for o in range(1, N):
         logit_x.start(o, logit_all.at[me])
     transpose_features(txt, txt_t, 0, rows_t)
-    for i in range(1, L):
-        transpose_features(img, img_t, i * PI, PI)
-    own = logit_all[me]
-    row_top = jnp.max(jnp.max(own, axis=0), axis=0, keepdims=True)
-    row_exp = jnp.exp(own - row_top[None])
-    row_prob = row_exp / jnp.sum(jnp.sum(row_exp, axis=0), axis=0, keepdims=True)[None]
-    caption = lax.broadcasted_iota(jnp.int32, (N, 8, 128), 0) * L + lax.broadcasted_iota(
-        jnp.int32, (N, 8, 128), 1
-    )
-    lanes = lax.broadcasted_iota(jnp.int32, (N, 8, 128), 2)
-    target = jnp.zeros((N, 8, 128), F32)
+    owner, image = lax.div(lane, L), lax.rem(lane, L)
+
+    def over_images(value, reduce, fill):
+        out = value
+        for j in range(N):
+            mine = owner == j
+            total = reduce(jnp.where(mine, value, fill), axis=1, keepdims=True)
+            out = jnp.where(mine, total, out)
+        return out
+
+    row_prob = jnp.zeros((8, 128), F32)
+    target = jnp.zeros((8, 128), F32)
     for i in range(L):
-        target = jnp.where((lanes == i) & (caption == pairs[0, me * L + i]), 1.0, target)
+        mine = image == i
+        values = jnp.where(mine, tile, LOW)
+        row_top = jnp.max(jnp.max(values, axis=1, keepdims=True), axis=0, keepdims=True)
+        row_exp = jnp.exp(values - row_top)
+        row_sum = jnp.sum(jnp.sum(row_exp, axis=1, keepdims=True), axis=0, keepdims=True)
+        row_prob = jnp.where(mine, row_exp / row_sum, row_prob)
+        hit = mine & (owner * L + line == pairs[0, me * L + i])
+        target = jnp.where(hit, 1.0, target)
     for o in range(1, N):
         logit_x.take(o)
     everyone = logit_all[...]
-    col_top = jnp.max(jnp.max(everyone, axis=0), axis=-1, keepdims=True)
-    col_sum = jnp.sum(
-        jnp.sum(jnp.exp(everyone - col_top[None]), axis=0), axis=-1, keepdims=True
-    )
-    col_prob = jnp.exp(own - col_top) / col_sum
+    col_top = over_images(jnp.max(everyone, axis=0), jnp.max, LOW)
+    col_sum = over_images(jnp.sum(jnp.exp(everyone - col_top[None]), axis=0), jnp.sum, 0.0)
+    col_prob = jnp.exp(tile - col_top) / col_sum
     pair_grad = (row_prob + col_prob - 2.0 * target) * (PAIR_SCALE / (2.0 * N * L * PI))
-    own_logits = logit_all.at[me]
     logit_x.finish()
-    own_logits[...] = pair_grad
 
     term_x = Exchange(me, N, on_neg, term_in, term_s, term_r)
     for o in list(range(1, N)) + [0]:
         j = term_x.peer(o) if o else me
-        pair = own_logits[j]
         spread = jnp.concatenate(
-            [jnp.broadcast_to(pair[:, i:i + 1], (8, PI)) for i in range(L)], axis=1
+            [
+                jnp.broadcast_to(
+                    jnp.sum(jnp.where(lane == j * L + i, pair_grad, 0.0), axis=1, keepdims=True),
+                    (8, PI),
+                )
+                for i in range(L)
+            ],
+            axis=1,
         )
         factor = spread / total[j]
         shares = []
@@ -334,11 +345,11 @@
     plane_send(1)
     ft[...] = nt(txt_back[...], wt[...]).astype(BF)
     save(1, ft, ft_hbm)
-    full_send(0)
     for i in range(1, L):
         rows = slice(i * PI, (i + 1) * PI)
         fi[rows, :] = nt(img_back[rows, :], wi[...]).astype(BF)
     save(0, fi, fi_hbm)
+    full_send(0)
     ring_send(1)
     result(0, gi_hbm)
     full_send(1)
@@ -385,7 +396,7 @@
         vmem((rows_i, W), F32), vmem((rows_i, 1), F32), vmem((rows_i, W), BF),
         vmem((rows_t, W), F32), vmem((rows_t, 1), F32),
         vmem((N, rows_t, W), BF), vmem((N, rows_t, rows_i), F32), vmem((N, 8, rows_i), F32),
-        vmem((N, N, 8, 128), F32), vmem((N, rows_t, rows_i), BF),
+        vmem((N, 8, 128), F32), vmem((N, rows_t, rows_i), BF),
         vmem((N, rows_t, W), BF), vmem((rows_t, W), F32), vmem((N, rows_t, W), BF),
         vmem((rows_i, W), BF), vmem((rows_t, W), BF),
         vmem((2, H, r, W), F32), vmem((2, H, r, W), BF), vmem((2, H, r, W), BF),

time: 41.6 us -> 41.3 us (level)
  no operation moved by 1% of the time
where the time goes in v1:
time: 41.3 us; the launch traced here: 41.1 us
  Pallas kernels  40.5 us (98%)
  between operations  0.64 us (2%)
    pallas_call x1, Pallas kernels, shards(): pl.pallas_call(functools.partial(kernel, (L, PI, T, D, W, N, n_dp)), out_...  38.1 us
    pallas_call x1, Pallas kernels, shards(): pl.pallas_call(write_out, out_shape=shapes, in_specs=[pl.BlockSpec(memory...  2.36 us

profile of v1, /device:TPU:0, one launch (start us, length us, event | category | flops | bytes accessed | tf_op | source)
XLA Modules:
  0.0 41.1 jit_solution(15715533507308783150)
XLA Ops:
  0.6 38.1 %shard_map.93 = (bf16[512,1024]{1,0:T(8,128)(2,1)}, bf16[128,1024]{1,0:T(8,128)(2,1)}, f32[128,256]{1,0:T(8,128)}, f32[128,256]{1,0:T(8,128)}) custom-call(bf16[512,1024]{1,0:T(8,128)(2,1)} %bitcast.4, bf16[128,1024]{1,0:T(8,128)(2,1)} %bitcast.5, bf16[1024,256]{1,0:T(8,128)(2,1)} %wi_hbm.1, bf16[1024,256]{1,0:T(8,128)(2,1)} %wt_hbm.1, s32[2]{0:T(128)} %cap.1, ...), custom_call_target="tpu_custom_call" | custom-call | tf_op jit(solution)/shard_map/pallas_call | solution.py:418
  38.8 2.4 %shard_map.94 = (bf16[512,1024]{1,0:T(8,128)(2,1)}, bf16[128,1024]{1,0:T(8,128)(2,1)}, f32[128,256]{1,0:T(8,128)}, f32[128,256]{1,0:T(8,128)}) custom-call(bf16[512,1024]{1,0:T(8,128)(2,1)} %get-tuple-element.12.refs_0_, bf16[128,1024]{1,0:T(8,128)(2,1)} %get-tuple-element.13.refs_1_, f32[128,256]{1,0:T(8,128)} %get-tuple-element.14.refs_2_, ...), custom_call_target="tpu_custom_call" | custom-call | tf_op jit(solution)/shard_map/pallas_call | solution.py:436

commit v2 on v1

--- a/solution.py
+++ b/solution.py
@@ -85,7 +85,7 @@
     img_unit, img_inv, img_half, txt_unit, txt_inv,
     text_all, expo, total, logit_all, sg, terms, own_term, term_in,
     img_back, txt_back, wg, core_out, core_in, plane_out, plane_own, plane_in,
-    part, part_out, ring_in, full, fi, ft, grads,
+    part, part_out, ring_in, wide_in, full, fi, ft, grads,
     load_sem, save_sem,
     text_s, text_r, logit_s, logit_r, term_s, term_r,
     core_s, core_r, plane_s, plane_r, ring_s, ring_r, full_s, full_r,
@@ -279,7 +279,9 @@
     planes = [
         Exchange(chip, H, on_plane, plane_in.at[m], plane_s.at[m], plane_r.at[m], line=False) for m in range(2)
     ]
-    rings = [Exchange(me, N, on_neg, ring_in.at[m], ring_s.at[m], ring_r.at[m]) for m in range(2)]
+    splits = (split, False)
+    slots = (ring_in if split else wide_in.at[0], wide_in.at[1])
+    rings = [Exchange(me, N, on_neg, slots[m], ring_s.at[m], ring_r.at[m]) for m in range(2)]
     fulls = [Exchange(me, N, on_neg, full.at[m], full_s.at[m], full_r.at[m]) for m in range(2)]
 
     def plane_send(m):
@@ -294,22 +296,22 @@
         value = plane_own[m]
         for o in range(1, H):
             value = value + plane_in[m, planes[m].take(o)].astype(F32)
-        if split:
+        if splits[m]:
             value = value.reshape(N, rr, W)
             part[m] = value
             part_out[m] = value.astype(BF)
             for o in range(1, N):
                 rings[m].start(o, part_out.at[m, rings[m].peer(o)])
         else:
-            ring_in[m, me] = value.astype(BF)
-            for o in range(1, N):
-                rings[m].start(o, ring_in.at[m, me])
+            wide_in[m, me] = value.astype(BF)
+            for o in range(1, N):
+                rings[m].start(o, wide_in.at[m, me])
 
     def full_send(m):
-        if split:
+        if splits[m]:
             value = part[m, me]
             for o in range(1, N):
-                value = value + ring_in[m, rings[m].take(o)].astype(F32)
+                value = value + ring_in[rings[m].take(o)].astype(F32)
             full[m, me] = value.astype(BF)
             for o in range(1, N):
                 fulls[m].start(o, full.at[m, me])
@@ -322,14 +324,14 @@
         saves.append(copy)
 
     def result(m, out):
-        if split:
+        if splits[m]:
             for o in range(1, N):
                 fulls[m].take(o)
             grads[m] = full[m].astype(F32).reshape(r, W)
         else:
             for o in range(1, N):
                 rings[m].take(o)
-            grads[m] = jnp.sum(ring_in[m].astype(F32), axis=0)
+            grads[m] = jnp.sum(wide_in[m].astype(F32), axis=0)
         save(2 + m, grads.at[m], out)
 
     weight_grad(0, img_t, img_back)
@@ -402,7 +404,7 @@
         vmem((2, H, r, W), F32), vmem((2, H, r, W), BF), vmem((2, H, r, W), BF),
         vmem((2, H, r, W), BF), vmem((2, r, W), F32), vmem((2, H, r, W), BF),
         vmem((2, N, rr, W), F32), vmem((2, N, rr, W), BF),
-        vmem((2, N, rr, W), BF), vmem((2, N, rr, W), BF),
+        vmem((N, rr, W), BF), vmem((2, N, r, W), BF), vmem((2, N, rr, W), BF),
         vmem((rows_i, D), BF), vmem((rows_t, D), BF), vmem((2, r, W), F32),
         dma((4,)), dma((4,)),
         dma((N,)), dma((N,)), dma((N,)), dma((N,)), dma((N,)), dma((N,)),

time: 41.3 us -> 40.5 us (0.981)
  Pallas kernels: 40.5 us -> 39.6 us
    pallas_call x1, Pallas kernels: 38.1 us -> 37.3 us  [shards(): pl.pallas_call(functools.partial(kernel, (L, PI, T, D, W, N, n_dp)), out_...]
where the time goes in v2:
time: 40.5 us; the launch traced here: 40.3 us
  Pallas kernels  39.6 us (98%)
  between operations  0.64 us (2%)
    pallas_call x1, Pallas kernels, shards(): pl.pallas_call(functools.partial(kernel, (L, PI, T, D, W, N, n_dp)), out_...  37.3 us
    pallas_call x1, Pallas kernels, shards(): pl.pallas_call(write_out, out_shape=shapes, in_specs=[pl.BlockSpec(memory...  2.36 us

profile of v2, /device:TPU:0, one launch (start us, length us, event | category | flops | bytes accessed | tf_op | source)
XLA Modules:
  0.0 40.3 jit_solution(13146810971270016806)
XLA Ops:
  0.6 37.3 %shard_map.93 = (bf16[512,1024]{1,0:T(8,128)(2,1)}, bf16[128,1024]{1,0:T(8,128)(2,1)}, f32[128,256]{1,0:T(8,128)}, f32[128,256]{1,0:T(8,128)}) custom-call(bf16[512,1024]{1,0:T(8,128)(2,1)} %bitcast.4, bf16[128,1024]{1,0:T(8,128)(2,1)} %bitcast.5, bf16[1024,256]{1,0:T(8,128)(2,1)} %wi_hbm.1, bf16[1024,256]{1,0:T(8,128)(2,1)} %wt_hbm.1, s32[2]{0:T(128)} %cap.1, ...), custom_call_target="tpu_custom_call" | custom-call | tf_op jit(solution)/shard_map/pallas_call | solution.py:420
  37.9 2.4 %shard_map.94 = (bf16[512,1024]{1,0:T(8,128)(2,1)}, bf16[128,1024]{1,0:T(8,128)(2,1)}, f32[128,256]{1,0:T(8,128)}, f32[128,256]{1,0:T(8,128)}) custom-call(bf16[512,1024]{1,0:T(8,128)(2,1)} %get-tuple-element.12.refs_0_, bf16[128,1024]{1,0:T(8,128)(2,1)} %get-tuple-element.13.refs_1_, f32[128,256]{1,0:T(8,128)} %get-tuple-element.14.refs_2_, ...), custom_call_target="tpu_custom_call" | custom-call | tf_op jit(solution)/shard_map/pallas_call | solution.py:438
